TPU v7x, 32 devices: a whole 2x2x4 slice. The times are simulated.
32 devices in a mesh: groups: 2 (over x), tensor: 4 (over y, core), dp: 4 (over z).
Axes of the slice: x: 2, y: 2, z: 4, core: 2. Of those that a mesh axis runs over, the one named last changes fastest.
Arguments:
- gate_pre: bfloat16 [2048, 14336], P(('groups', 'dp'), 'tensor'), parts along dimension 0, may hold values from -6 to 6
- up_pre: bfloat16 [2048, 14336], P(('groups', 'dp'), 'tensor'), parts along dimension 0, may hold values from -6 to 6
- grad_out: bfloat16 [2048, 4096], P(('groups', 'dp', 'tensor')), parts along dimension 0, may hold values from -6 to 6
- down_weight: bfloat16 [14336, 4096], P('tensor'), may hold values from -0.046875 to 0.046875
- delta_values: bfloat16 [64, 128, 128], P(('groups', 'tensor')), parts along dimension 0, may hold values from -0.1796875 to 0.1796875
- delta_rows: int32 [64], P(('groups', 'tensor')), parts along dimension 0, may hold values from 0 to 111, as said below
- delta_cols: int32 [64], P(('groups', 'tensor')), parts along dimension 0, may hold values from 0 to 31
- delta_owner: int32 [64], P(('groups', 'tensor')), parts along dimension 0, may hold values from 0 to 3, as said below
Outputs:
- grad_gate: bfloat16 [2048, 14336], P(('groups', 'dp'), 'tensor'), parts along dimension 0
- grad_up: bfloat16 [2048, 14336], P(('groups', 'dp'), 'tensor'), parts along dimension 0
- delta_grad: float32 [8, 16, 128, 128], P(('groups', 'tensor'), 'dp'), parts along dimension 0
There are 2 independent parts, one for each index of `groups`. A program takes and returns all parts, laid end to end along the dimension named above; an argument that names none is the same for every part. Nothing has to cross between parts.
Inputs may be any that keep to these rules, and one draw needn't show every extreme that they name: Block k lies in the hidden units of tensor shard k // 8: delta_rows[k] // 28 == k // 8. `delta_owner`: among the 8 blocks of one tensor shard at most 4 have one owner, and in every shard some owner has exactly 4.
All inputs are finite; a program needn't handle non-finite values.
Results may differ from a plain program's by a relative error of at most 0.0036.
Values may be sent and summed in bfloat16 or wider, within the bound.
A program may use at most 128 MiB of HBM per device.

v0:
```python
import jax
import jax.numpy as jnp
from jax import lax
from jax.sharding import PartitionSpec as P

CAP = 4


def local(
    gate_pre, up_pre, grad_out, down_weight, delta_values, delta_rows, delta_cols, delta_owner
):
    tok_rows, ff_local = gate_pre.shape
    blocks = delta_values.shape[0]
    block_size = delta_values.shape[1]
    row_blocks = ff_local // block_size
    gate_val = gate_pre.astype(jnp.float32)
    up_val = up_pre.astype(jnp.float32)
    sigma_val = jax.nn.sigmoid(gate_val)
    active = gate_val * sigma_val
    slope_val = sigma_val * (1.0 + gate_val * (1.0 - sigma_val))
    hidden = (active * up_val).astype(jnp.bfloat16)
    local_rows = delta_rows - lax.axis_index("tensor") * row_blocks
    row_starts = local_rows * block_size
    col_starts = delta_cols * block_size
    same_place = (
        (local_rows[:, None] == local_rows[None, :]) & (delta_cols[:, None] == delta_cols[None, :])
    ).astype(jnp.float32)
    summed_delta = jnp.einsum(
        "kl,lij->kij",
        same_place,
        delta_values.astype(jnp.float32),
        precision=lax.Precision.HIGHEST,
        preferred_element_type=jnp.float32,
    )

    def frozen_tile(pair):
        return lax.dynamic_slice(down_weight, (pair[0], pair[1]), (block_size, block_size))

    base_tiles = lax.map(frozen_tile, (row_starts, col_starts))
    new_tiles = (base_tiles.astype(jnp.float32) + summed_delta).astype(jnp.bfloat16)

    def place_tile(index, matrix):
        return lax.dynamic_update_slice(
            matrix, new_tiles[index], (row_starts[index], col_starts[index])
        )

    effective = lax.fori_loop(0, blocks, place_tile, down_weight)
    scale_val = float(tok_rows * lax.axis_size("dp")) ** (-0.5)
    gathered = lax.all_gather(grad_out, "tensor", axis=0, tiled=True)
    grad_hidden = lax.dot_general(
        gathered, effective, (((1,), (1,)), ((), ())), preferred_element_type=jnp.float32
    )
    gate_rows = (grad_hidden * up_val * slope_val).astype(jnp.bfloat16)
    upper_rows = (grad_hidden * active).astype(jnp.bfloat16)

    def block_term(pair):
        left = lax.dynamic_slice_in_dim(hidden, pair[0], block_size, 1)
        right = lax.dynamic_slice_in_dim(gathered, pair[1], block_size, 1)
        return lax.dot_general(
            left, right, (((0,), (0,)), ((), ())), preferred_element_type=jnp.float32
        )

    terms = lax.map(block_term, (row_starts, col_starts))
    flattened = (terms * scale_val).reshape(blocks, block_size * block_size)
    dp_count = lax.axis_size("dp")
    block_ids = jnp.arange(blocks)
    earlier = (delta_owner[:, None] == delta_owner[None, :]) & (
        block_ids[None, :] < block_ids[:, None]
    )
    rank_index = jnp.sum(earlier.astype(jnp.int32), axis=1)
    slot_index = delta_owner * CAP + rank_index
    placing = (jnp.arange(dp_count * CAP)[:, None] == slot_index[None, :]).astype(jnp.float32)
    buffered = jnp.dot(
        placing, flattened, precision=lax.Precision.HIGHEST, preferred_element_type=jnp.float32
    )
    own_blocks = lax.psum_scatter(buffered, "dp", scatter_dimension=0, tiled=True)
    return (gate_rows, upper_rows, own_blocks.reshape(1, CAP, block_size, block_size))


def solution(mesh):
    placed = (
        P(("groups", "dp"), "tensor"),
        P(("groups", "dp"), "tensor"),
        P(("groups", "dp", "tensor"), None),
        P("tensor", None),
        P(("groups", "tensor"), None, None),
        P(("groups", "tensor")),
        P(("groups", "tensor")),
        P(("groups", "tensor")),
    )
    return jax.shard_map(
        local,
        mesh=mesh,
        in_specs=placed,
        out_specs=(
            P(("groups", "dp"), "tensor"),
            P(("groups", "dp"), "tensor"),
            P(("groups", "tensor"), "dp", None, None),
        ),
        check_vma=False,
    )
```

profile of v0, /device:TPU:11, one launch (start us, length us, event | category | flops | bytes accessed | tf_op | source)
XLA Modules:
  0.0 280.5 jit_solution(17677542474704156227)
XLA Ops:
  7.2 20.0 %copy.64 = bf16[3584,4096]{1,0:T(8,128)(2,1)} copy(bf16[3584,4096]{1,0:T(8,128)(2,1)} %param.17) | data formatting | bytes 58720256
  27.4 48.6 %while.33 = (s32[]{:T(128)}, bf16[8,128,128]{2,1,0:T(8,128)(2,1)S(1)}, s32[8]{0:T(128)S(1)}, s32[8]{0:T(128)S(1)}, bf16[3584,4096]{1,0:T(8,128)(2,1)}, /*index=5*/s32[]{:T(128)}, s32[]{:T(128)}, s32[]{:T(128)}, s32[]{:T(128)}) while((s32[]{:T(128)}, bf16[8,128,128]{2,1,0:T(8,128)(2,1)S(1)}, s32[8]{0:T(128)S(1)}, s32[8]{0:T(128)S(1)}, ...), condition=%wide.region_1.2_spmd, body=%wide.region_0.1_spmd.sunk | while | flops 8 | bytes 65733 | solution.py:39
  76.5 2.3 copy.24
  78.8 3.9 %copy.25 = bf16[256,3584]{0,1:T(8,128)(2,1)} copy(bf16[256,3584]{1,0:T(8,128)(2,1)} %param.14) | data formatting | bytes 3670016 | tf_op args[0]
  82.9 66.9 %while.34 = (s32[]{:T(128)}, bf16[3584,4096]{1,0:T(8,128)(2,1)}, bf16[8,128,128]{2,1,0:T(8,128)(2,1)S(1)}, s32[8]{0:T(128)S(1)}, s32[8]{0:T(128)S(1)}, /*index=5*/s32[]{:T(128)}, s32[]{:T(128)}, s32[]{:T(128)}, s32[]{:T(128)}) while((s32[]{:T(128)}, bf16[3584,4096]{1,0:T(8,128)(2,1)}, bf16[8,128,128]{2,1,0:T(8,128)(2,1)S(1)}, s32[8]{0:T(128)S(1)}, ...), condition=%wide.region_3.4_spmd, body=%wide.region_2.3_spmd.sunk | while | flops 8 | bytes 131265 | solution.py:47
  88.4 2.9 %dynamic_update_slice.21 = bf16[3584,4096]{1,0:T(8,128)(2,1)} dynamic-update-slice(bf16[3584,4096]{1,0:T(8,128)(2,1)} %get-tuple-element.365, bf16[128,128]{1,0:T(8,128)(2,1)S(1)} %dynamic-slice_bitcast_fusion.3, s32[]{:T(128)S(6)} %select_n.41, s32[]{:T(128)S(6)} %select_n.42) | dynamic-update-slice | bytes 65540 | tf_op jit(solution)/shard_map/while/body/eval_jaxpr/dynamic_update_slice | solution.py:43
  96.8 2.9 %dynamic_update_slice.21 = bf16[3584,4096]{1,0:T(8,128)(2,1)} dynamic-update-slice(bf16[3584,4096]{1,0:T(8,128)(2,1)} %get-tuple-element.365, bf16[128,128]{1,0:T(8,128)(2,1)S(1)} %dynamic-slice_bitcast_fusion.3, s32[]{:T(128)S(6)} %select_n.41, s32[]{:T(128)S(6)} %select_n.42) | dynamic-update-slice | bytes 65540 | tf_op jit(solution)/shard_map/while/body/eval_jaxpr/dynamic_update_slice | solution.py:43
  105.2 2.8 %dynamic_update_slice.21 = bf16[3584,4096]{1,0:T(8,128)(2,1)} dynamic-update-slice(bf16[3584,4096]{1,0:T(8,128)(2,1)} %get-tuple-element.365, bf16[128,128]{1,0:T(8,128)(2,1)S(1)} %dynamic-slice_bitcast_fusion.3, s32[]{:T(128)S(6)} %select_n.41, s32[]{:T(128)S(6)} %select_n.42) | dynamic-update-slice | bytes 65540 | tf_op jit(solution)/shard_map/while/body/eval_jaxpr/dynamic_update_slice | solution.py:43
  113.5 2.9 %dynamic_update_slice.21 = bf16[3584,4096]{1,0:T(8,128)(2,1)} dynamic-update-slice(bf16[3584,4096]{1,0:T(8,128)(2,1)} %get-tuple-element.365, bf16[128,128]{1,0:T(8,128)(2,1)S(1)} %dynamic-slice_bitcast_fusion.3, s32[]{:T(128)S(6)} %select_n.41, s32[]{:T(128)S(6)} %select_n.42) | dynamic-update-slice | bytes 65540 | tf_op jit(solution)/shard_map/while/body/eval_jaxpr/dynamic_update_slice | solution.py:43
  121.9 2.9 %dynamic_update_slice.21 = bf16[3584,4096]{1,0:T(8,128)(2,1)} dynamic-update-slice(bf16[3584,4096]{1,0:T(8,128)(2,1)} %get-tuple-element.365, bf16[128,128]{1,0:T(8,128)(2,1)S(1)} %dynamic-slice_bitcast_fusion.3, s32[]{:T(128)S(6)} %select_n.41, s32[]{:T(128)S(6)} %select_n.42) | dynamic-update-slice | bytes 65540 | tf_op jit(solution)/shard_map/while/body/eval_jaxpr/dynamic_update_slice | solution.py:43
  130.2 2.8 %dynamic_update_slice.21 = bf16[3584,4096]{1,0:T(8,128)(2,1)} dynamic-update-slice(bf16[3584,4096]{1,0:T(8,128)(2,1)} %get-tuple-element.365, bf16[128,128]{1,0:T(8,128)(2,1)S(1)} %dynamic-slice_bitcast_fusion.3, s32[]{:T(128)S(6)} %select_n.41, s32[]{:T(128)S(6)} %select_n.42) | dynamic-update-slice | bytes 65540 | tf_op jit(solution)/shard_map/while/body/eval_jaxpr/dynamic_update_slice | solution.py:43
  138.6 2.9 %dynamic_update_slice.21 = bf16[3584,4096]{1,0:T(8,128)(2,1)} dynamic-update-slice(bf16[3584,4096]{1,0:T(8,128)(2,1)} %get-tuple-element.365, bf16[128,128]{1,0:T(8,128)(2,1)S(1)} %dynamic-slice_bitcast_fusion.3, s32[]{:T(128)S(6)} %select_n.41, s32[]{:T(128)S(6)} %select_n.42) | dynamic-update-slice | bytes 65540 | tf_op jit(solution)/shard_map/while/body/eval_jaxpr/dynamic_update_slice | solution.py:43
  146.9 2.9 %dynamic_update_slice.21 = bf16[3584,4096]{1,0:T(8,128)(2,1)} dynamic-update-slice(bf16[3584,4096]{1,0:T(8,128)(2,1)} %get-tuple-element.365, bf16[128,128]{1,0:T(8,128)(2,1)S(1)} %dynamic-slice_bitcast_fusion.3, s32[]{:T(128)S(6)} %select_n.41, s32[]{:T(128)S(6)} %select_n.42) | dynamic-update-slice | bytes 65540 | tf_op jit(solution)/shard_map/while/body/eval_jaxpr/dynamic_update_slice | solution.py:43
  149.8 17.5 %multiply_convert_fusion = (bf16[256,3584]{0,1:T(8,128)(2,1)}, bf16[256,3584]{0,1:T(8,128)(2,1)}, bf16[256,3584]{0,1:T(8,128)(2,1)}) fusion(bf16[256,3584]{0,1:T(8,128)(2,1)} %copy.25, bf16[256,3584]{0,1:T(8,128)(2,1)S(1)} %copy-done.3, bf16[3584,4096]{1,0:T(8,128)(2,1)} %get-tuple-element.157, bf16[256,4096]{1,0:T(8,128)(2,1)} %all-gather.2.cloned.1.call-done), kind=kOutput, calls=%fused_computation.21 | convolution fusion | flops 7531790336 | bytes 40632320 | tf_op jit(solution)/shard_map/dot_general | solution.py:50
  167.3 50.0 %while.35 = (s32[]{:T(128)}, f32[8,128,128]{2,1,0:T(8,128)S(1)}, s32[8]{0:T(128)S(1)}, bf16[256,3584]{0,1:T(8,128)(2,1)}, s32[8]{0:T(128)S(1)}, /*index=5*/bf16[...) while((s32[]{:T(128)}, f32[8,128,128]{2,1,0:T(8,128)S(1)}, s32[8]{0:T(128)S(1)}, ...), condition=%wide.region_6.7_spmd, body=%wide.region_5.6_spmd.sunk | while | flops 8388616 | bytes 197321 | solution.py:63
  172.3 1.2 fusion.34
  178.6 1.2 fusion.34
  184.8 1.2 fusion.34
  191.1 1.2 fusion.34
  209.9 1.2 fusion.34
  217.3 1.8 fusion.13
  220.4 3.8 %copy.27 = bf16[256,3584]{1,0:T(8,128)(2,1)} copy(bf16[256,3584]{0,1:T(8,128)(2,1)} %get-tuple-element.226) | data formatting | bytes 3670016
  224.3 3.8 %copy.28 = bf16[256,3584]{1,0:T(8,128)(2,1)} copy(bf16[256,3584]{0,1:T(8,128)(2,1)} %get-tuple-element.225) | data formatting | bytes 3670016
  228.1 43.8 %all-reduce.3.cloned.1.call-done = f32[16,16384]{1,0:T(8,128)} async-done(((f32[16,16384]{1,0:T(8,128)}), f32[16,16384]{1,0:T(8,128)}) %all-reduce.3.cloned.1.call-update) | async-done | bytes 1048592
  (99 shorter events, 44.2 us)
Async XLA Ops:
  7.2 68.9 %copy-start = (bf16[8,128,128]{2,1,0:T(8,128)(2,1)S(1)}, bf16[8,128,128]{2,1,0:T(8,128)(2,1)}, u32[]{:S(2)}) copy-start(bf16[8,128,128]{2,1,0:T(8,128)(2,1)} %param.18) | copy-start | bytes 786436
  7.2 20.2 %copy-start.5 = (s32[8]{0:T(128)S(1)}, s32[8]{0:T(128)}, u32[]{:S(2)}) copy-start(s32[8]{0:T(128)} %param.19) | copy-start | bytes 100
  7.2 20.2 %copy-start.4 = (s32[8]{0:T(128)S(1)}, s32[8]{0:T(128)}, u32[]{:S(2)}) copy-start(s32[8]{0:T(128)} %param.20) | copy-start | bytes 100
  7.2 142.6 %all-gather.2.cloned.1.call-start = ((), (), s32[]{:S(2)}) async-start(), calls=%async_computation | async-start | bytes 2621440 | tf_op jit(solution)/shard_map/all_gather | solution.py:49
  27.3 49.2 %copy-start.2 = (bf16[256,3584]{1,0:T(8,128)(2,1)S(1)}, bf16[256,3584]{1,0:T(8,128)(2,1)}, u32[]{:S(2)}) copy-start(bf16[256,3584]{1,0:T(8,128)(2,1)} %param.15) | copy-start | bytes 5505028
  27.3 244.6 %all-reduce.3.cloned.1.call-start = ((), (), s32[]{:S(2)}) async-start(), calls=%async_computation.1 | async-start | bytes 2097152
  76.5 6.2 %copy-start.6 = (s32[8]{0:T(128)S(1)}, s32[8]{0:T(128)}, u32[]{:S(2)}) copy-start(s32[8]{0:T(128)} %param.21) | copy-start | bytes 100
  78.8 71.0 %copy-start.3 = (bf16[256,3584]{0,1:T(8,128)(2,1)S(1)}, bf16[256,3584]{0,1:T(8,128)(2,1)}, u32[]{:S(2)}) copy-start(bf16[256,3584]{0,1:T(8,128)(2,1)} %copy.24) | copy-start | bytes 5505028
  167.3 51.9 %copy-start.7 = (u32[32]{0:T(128)S(1)}, u32[32]{0:T(128)}, u32[]{:S(2)}) copy-start(u32[32]{0:T(128)} %constant.81) | copy-start | bytes 388
  220.4 53.3 %copy-start.1 = (bf16[8,128,128]{2,1,0:T(8,128)(2,1)S(1)}, bf16[8,128,128]{2,1,0:T(8,128)(2,1)}, u32[]{:S(2)}) copy-start(bf16[8,128,128]{2,1,0:T(8,128)(2,1)} %param.18) | copy-start | bytes 786436
Sparse Core Ops, SparseCore 0:
  27.4 24.1 all-gather.1
  219.3 52.5 all-reduce.2
where the time goes:
time: 286 us; the launch traced here: 281 us
  local copies, waits for them, and re-layouts  96.8 us (34%)
  loops' own time  95.8 us (33%)
  waiting for transfers between devices  43.8 us (15%)
  matrix products  29 us (10%)
  between operations  14.9 us (5%)
    unnamed x3, waiting for transfers between devices  43.8 us
    unnamed x24, local copies, waits for them, and re-layouts  36.3 us
    another operation x1, loops' own time, local(): effective = lax.fori_loop(0, blocks, place_tile, down_weight)  33.3 us
    another operation x1, loops' own time, local(): terms = lax.map(block_term, (row_starts, col_starts))  31.3 us
    another operation x1, loops' own time, local(): base_tiles = lax.map(frozen_tile, (row_starts, col_starts))  31.2 us
    dynamic_update_slice x8, local copies, waits for them, and re-layouts, place_tile(): lax.dynamic_update_slice(matrix, new_tiles[index], (row_starts[index], co...  22.8 us
    dynamic_slice x32, local copies, waits for them, and re-layouts, local(): base_tiles = lax.map(frozen_tile, (row_starts, col_starts))  18.8 us
    dot_general x1, matrix products, local(): lax.dot_general(gathered, effective, (((1,), (1,)), ((), ())), preferred_...  17.5 us
  transfers between devices with their start and end apart: 2, of which 1 were waited for; matrix products, arithmetic and copies ran while one was open for 24% of the time, Pallas kernels for 0%

commit v1 on v0

v1 whole, which is shorter than its diff:
```python
import functools

import jax
import jax.numpy as jnp
from jax import lax
from jax.experimental import pallas as pl
from jax.experimental.pallas import tpu as pltpu
from jax.sharding import PartitionSpec as P

CAP = 4
CORES = 2
MESH = pl.DeviceIdType.MESH
F32 = jnp.float32
BF16 = jnp.bfloat16
NT = (((1,), (1,)), ((), ()))


def widest(total, options):
    for option in options:
        if total % option == 0:
            return option
    return total


def kernel(
    n_t, n_d, rows_ref, cols_ref, owner_ref, gate_hbm, up_hbm, go_hbm, w_hbm, dv_ref,
    gg_hbm, gu_hbm, dg_hbm,
    gate_v, up_v, slope_v, act_v, go_v, w_v, acc_v, all_hid_v, go_col_v, hid_v, term_v, send_v, recv_v, corr_v, comb_v, own_v,
    in_sem, w_sem, out_sem, dg_sem, sib_sem, cs_sem, cr_sem, fs_sem, fr_sem, rs_sem, rr_sem,
):
    tok, ff = gate_v.shape
    depth = w_v.shape[1]
    shard_tok = go_hbm.shape[0]
    blocks, side = dv_ref.shape[0], dv_ref.shape[1]
    n_y = n_t // CORES
    chunks = w_sem.shape[0]
    wide = depth // chunks
    tile = widest(ff, (512, 256, 128))
    tiles = ff // tile
    me_t = lax.axis_index("tensor")
    me_d = lax.axis_index("dp")
    core = lax.rem(me_t, CORES)
    me_y = lax.div(me_t, CORES)
    sibling = me_y * CORES + (1 - core)

    def on_y(offset):
        return lax.rem(me_y + offset + n_y, n_y) * CORES + core

    def tokens_of(t):
        return pl.ds(pl.multiple_of(t * shard_tok, shard_tok), shard_tok)

    gate_in = pltpu.make_async_copy(gate_hbm, gate_v, in_sem.at[0])
    up_in = pltpu.make_async_copy(up_hbm, up_v, in_sem.at[1])
    go_in = pltpu.make_async_copy(go_hbm, go_v.at[tokens_of(me_t)], in_sem.at[2])
    gate_in.start()
    up_in.start()
    go_in.start()
    w_in = []
    for c in range(chunks):
        span = pl.ds(c * wide, wide)
        w_in.append(pltpu.make_async_copy(w_hbm.at[:, span], w_v.at[:, span], w_sem.at[c]))
        w_in[-1].start()

    barrier = pltpu.get_barrier_semaphore()
    pl.semaphore_signal(barrier, inc=1, device_id={"tensor": sibling}, device_id_type=MESH)
    for off in range(1, n_y):
        pl.semaphore_signal(barrier, inc=1, device_id={"tensor": on_y(off)}, device_id_type=MESH)
    for off in range(1, n_d):
        peer = lax.rem(me_d + off, n_d)
        pl.semaphore_signal(barrier, inc=1, device_id={"dp": peer}, device_id_type=MESH)
    pl.semaphore_wait(barrier, 1 + (n_y - 1) + (n_d - 1))

    cross, forward = {}, {}
    for c in range(chunks):
        span = pl.ds(c * wide, wide)
        for off in range(1, n_y):
            cross[off, c] = pltpu.make_async_remote_copy(
                src_ref=go_hbm.at[:, span], dst_ref=go_v.at[tokens_of(me_t), span],
                send_sem=cs_sem.at[off - 1, c], recv_sem=cr_sem.at[off - 1, c],
                device_id={"tensor": on_y(off)}, device_id_type=MESH)
            cross[off, c].start()
    to_sibling = pltpu.make_async_remote_copy(
        src_ref=go_hbm, dst_ref=go_v.at[tokens_of(me_t)],
        send_sem=sib_sem.at[0], recv_sem=sib_sem.at[1],
        device_id={"tensor": sibling}, device_id_type=MESH)
    to_sibling.start()

    gate_in.wait()
    up_in.wait()
    strip = 64
    strips = tok // strip

    def factors(step, carry):
        rows = pl.ds(pl.multiple_of(lax.rem(step, strips) * strip, strip), strip)
        span = pl.ds(pl.multiple_of(lax.div(step, strips) * side, side), side)
        gate = gate_v[rows, span].astype(F32)
        sigma = jax.nn.sigmoid(gate)
        act = gate * sigma
        up = up_v[rows, span].astype(F32)
        act_v[rows, span] = act
        slope_v[rows, span] = up * (sigma * (1.0 + gate * (1.0 - sigma)))
        all_hid_v[lax.div(step, strips), rows] = (act * up).astype(BF16)
        return carry

    lax.fori_loop(0, strips * (ff // side), factors, 0, unroll=2)

    row = [lax.rem(rows_ref[k], ff // side) for k in range(blocks)]
    col = [cols_ref[k] for k in range(blocks)]
    owner = [owner_ref[k] for k in range(blocks)]
    slot = []
    for k in range(blocks):
        rank = jnp.int32(0)
        for k2 in range(k):
            rank = rank + (owner[k2] == owner[k]).astype(jnp.int32)
        slot.append(owner[k] * CAP + rank)

    first = []
    for k in range(blocks):
        alone = jnp.int32(1)
        for k2 in range(k):
            alone = alone * (1 - (row[k2] == row[k]).astype(jnp.int32))
        first.append(alone)

    def block_in(s):
        found = jnp.int32(blocks)
        for k in range(blocks):
            found = found + (slot[k] == s).astype(jnp.int32) * (k - blocks)
        return found

    for k in range(blocks):
        hid_v[k] = all_hid_v[row[k]].astype(F32).T.astype(BF16)

    def partial_sum(c, j):
        span = pl.ds(c * wide, wide)
        part = pl.ds(pl.multiple_of(j * tile, tile), tile)
        return lax.dot_general(go_v[:, span], w_v[part, span], NT, preferred_element_type=F32)

    def by_column(c):
        for i in range(c * wide // side, (c + 1) * wide // side):
            go_col_v[i] = go_v[:, i * side:(i + 1) * side]

    def chunk_step(c):
        by_column(c)
        w_in[c].wait()

        def body(j, carry):
            part = pl.ds(pl.multiple_of(j * tile, tile), tile)
            got = partial_sum(c, j)
            if c == 0:
                acc_v[:, part] = got
            else:
                acc_v[:, part] = acc_v[:, part] + got
            return carry

        lax.fori_loop(0, tiles, body, 0)

    for c in range(chunks):
        span = pl.ds(c * wide, wide)
        for off in range(1, n_y):
            cross[off, c].wait_recv()
            source = on_y(-off)
            forward[off, c] = pltpu.make_async_remote_copy(
                src_ref=go_v.at[tokens_of(source), span], dst_ref=go_v.at[tokens_of(source), span],
                send_sem=fs_sem.at[off - 1, c], recv_sem=fr_sem.at[off - 1, c],
                device_id={"tensor": sibling}, device_id_type=MESH)
            forward[off, c].start()
        if c == 0:
            go_in.wait()
            to_sibling.wait_recv()
        else:
            for off in range(1, n_y):
                forward[off, c - 1].wait_recv()
            chunk_step(c - 1)
    for off in range(1, n_y):
        forward[off, chunks - 1].wait_recv()
    by_column(chunks - 1)

    scale = float(tok * n_d) ** -0.5
    for k in range(blocks):
        term_v[k] = scale * jnp.dot(hid_v[k], go_col_v[col[k]], preferred_element_type=F32)
    term_v[blocks] = jnp.zeros((side, side), F32)
    for s in range(n_d * CAP):
        send_v[s] = term_v[block_in(s)].astype(BF16)
    scatter = []
    for off in range(1, n_d):
        peer = lax.rem(me_d + off, n_d)
        scatter.append(pltpu.make_async_remote_copy(
            src_ref=send_v.at[pl.ds(peer * CAP, CAP)], dst_ref=recv_v.at[off - 1],
            send_sem=rs_sem.at[off - 1], recv_sem=rr_sem.at[off - 1],
            device_id={"dp": peer}, device_id_type=MESH))
        scatter[-1].start()

    for k in range(blocks):
        corr_v[k] = lax.dot_general(go_col_v[col[k]], dv_ref[k], NT, preferred_element_type=F32)
    for k in range(blocks):
        total = corr_v[k]
        for k2 in range(blocks):
            if k2 != k:
                total = total + (row[k2] == row[k]).astype(jnp.int32).astype(F32) * corr_v[k2]
        comb_v[k] = total
    comb_v[blocks] = jnp.zeros((tok, side), F32)

    def outputs(j):
        part = pl.ds(pl.multiple_of(j * tile, tile), tile)
        return (pltpu.make_async_copy(gate_v.at[:, part], gg_hbm.at[:, part], out_sem.at[0, j]),
                pltpu.make_async_copy(up_v.at[:, part], gu_hbm.at[:, part], out_sem.at[1, j]))

    w_in[chunks - 1].wait()

    def last(j, carry):
        got = partial_sum(chunks - 1, j)
        for i in range(tile // side):
            part = pl.ds(pl.multiple_of(j * tile + i * side, side), side)
            which = j * (tile // side) + i
            found = jnp.int32(blocks)
            for k in range(blocks):
                found = found + first[k] * (row[k] == which).astype(jnp.int32) * (k - blocks)
            grad = got[:, i * side:(i + 1) * side] + acc_v[:, part] + comb_v[found]
            gate_v[:, part] = (grad * slope_v[:, part]).astype(BF16)
            up_v[:, part] = (grad * act_v[:, part]).astype(BF16)
        for copy in outputs(j):
            copy.start()
        return carry

    lax.fori_loop(0, tiles, last, 0)

    for i in range(CAP):
        own_v[0, i] = term_v[block_in(me_d * CAP + i)]
    for off in range(1, n_d):
        scatter[off - 1].wait_recv()
    for i in range(CAP):
        total = own_v[0, i]
        for off in range(1, n_d):
            total = total + recv_v[off - 1, i].astype(F32)
        own_v[0, i] = total
    dg_out = pltpu.make_async_copy(own_v, dg_hbm, dg_sem)
    dg_out.start()

    def drain(j, carry):
        for copy in outputs(j):
            copy.wait()
        return carry

    lax.fori_loop(0, tiles, drain, 0)
    for c in range(chunks):
        for off in range(1, n_y):
            cross[off, c].wait_send()
            forward[off, c].wait_send()
    to_sibling.wait_send()
    for copy in scatter:
        copy.wait_send()
    dg_out.wait()


def local(n_t, n_d, gate_pre, up_pre, grad_out, down_weight, delta_values, delta_rows, delta_cols, delta_owner):
    tok, ff = gate_pre.shape
    depth = down_weight.shape[1]
    blocks, side = delta_values.shape[0], delta_values.shape[1]
    chunks = 4
    n_y = n_t // CORES
    tiles = ff // widest(ff, (512, 256, 128))
    smem = pl.BlockSpec(memory_space=pltpu.SMEM)
    anywhere = pl.BlockSpec(memory_space=pl.ANY)
    vmem = pl.BlockSpec(memory_space=pltpu.VMEM)
    dma = pltpu.SemaphoreType.DMA
    return pl.pallas_call(
        functools.partial(kernel, n_t, n_d),
        out_shape=(
            jax.ShapeDtypeStruct((tok, ff), BF16),
            jax.ShapeDtypeStruct((tok, ff), BF16),
            jax.ShapeDtypeStruct((1, CAP, side, side), F32),
        ),
        in_specs=[smem] * 3 + [anywhere] * 4 + [vmem],
        out_specs=(anywhere, anywhere, anywhere),
        scratch_shapes=[
            pltpu.VMEM((tok, ff), BF16),
            pltpu.VMEM((tok, ff), BF16),
            pltpu.VMEM((tok, ff), F32),
            pltpu.VMEM((tok, ff), F32),
            pltpu.VMEM((tok, depth), BF16),
            pltpu.VMEM((ff, depth), BF16),
            pltpu.VMEM((tok, ff), F32),
            pltpu.VMEM((ff // side, tok, side), BF16),
            pltpu.VMEM((depth // side, tok, side), BF16),
            pltpu.VMEM((blocks, side, tok), BF16),
            pltpu.VMEM((blocks + 1, side, side), F32),
            pltpu.VMEM((n_d * CAP, side, side), BF16),
            pltpu.VMEM((n_d - 1, CAP, side, side), BF16),
            pltpu.VMEM((blocks, tok, side), F32),
            pltpu.VMEM((blocks + 1, tok, side), F32),
            pltpu.VMEM((1, CAP, side, side), F32),
            dma((3,)),
            dma((chunks,)),
            dma((2, tiles)),
            dma,
            dma((2,)),
            dma((n_y - 1, chunks)),
            dma((n_y - 1, chunks)),
            dma((n_y - 1, chunks)),
            dma((n_y - 1, chunks)),
            dma((n_d - 1,)),
            dma((n_d - 1,)),
        ],
        compiler_params=pltpu.CompilerParams(
            collective_id=0, has_side_effects=True, vmem_limit_bytes=60 * 2**20
        ),
    )(delta_rows, delta_cols, delta_owner, gate_pre, up_pre, grad_out, down_weight, delta_values)


def solution(mesh):
    placed = (
        P(("groups", "dp"), "tensor"),
        P(("groups", "dp"), "tensor"),
        P(("groups", "dp", "tensor"), None),
        P("tensor", None),
        P(("groups", "tensor"), None, None),
        P(("groups", "tensor")),
        P(("groups", "tensor")),
        P(("groups", "tensor")),
    )
    return jax.shard_map(
        functools.partial(local, mesh.shape["tensor"], mesh.shape["dp"]),
        mesh=mesh,
        in_specs=placed,
        out_specs=(
            P(("groups", "dp"), "tensor"),
            P(("groups", "dp"), "tensor"),
            P(("groups", "tensor"), "dp", None, None),
        ),
        check_vma=False,
    )
```

time: 286 us -> 43 us (0.15)
  the two profiles are of different devices: /device:TPU:11 before, /device:TPU:0 now
where the time goes in v1:
time: 43 us; the launch traced here: 42.9 us
  Pallas kernels  37.3 us (87%)
  local copies, waits for them, and re-layouts  4.92 us (11%)
  between operations  0.65 us (2%)
    pallas_call x1, Pallas kernels, local(): pl.pallas_call(functools.partial(kernel, n_t, n_d), out_shape=(jax.ShapeD...  37.3 us
    unnamed x7, local copies, waits for them, and re-layouts  4.92 us

profile of v1, /device:TPU:0, one launch (start us, length us, event | category | flops | bytes accessed | tf_op | source)
XLA Modules:
  0.0 42.9 jit_solution(3824764654260377896)
XLA Ops:
  0.6 37.3 %shard_map.103 = (bf16[256,3584]{1,0:T(8,128)(2,1)}, bf16[256,3584]{1,0:T(8,128)(2,1)}, f32[1,4,128,128]{3,2,1,0:T(8,128)}) custom-call(s32[8]{0:T(128)} %rows_ref.1, s32[8]{0:T(128)} %cols_ref.1, s32[8]{0:T(128)} %owner_ref.1, bf16[256,3584]{1,0:T(8,128)(2,1)} %gate_hbm.1, bf16[256,3584]{1,0:T(8,128)(2,1)} %up_hbm.1, bf16[64,4096]{1,0:T(8,128)(2,1)} %go_hbm.1, ...), custom_call_target="tpu_custom_call" | custom-call | tf_op jit(solution)/shard_map/pallas_call | solution.py:266
  37.9 0.0 copy-start
  38.0 3.0 %copy.14 = bf16[256,3584]{1,0:T(8,128)(2,1)} copy(bf16[256,3584]{1,0:T(8,128)(2,1)} %get-tuple-element.6) | data formatting | bytes 3670016
  40.9 0.0 copy-done
  40.9 0.0 copy-start.1
  40.9 1.2 %copy.15 = bf16[256,3584]{1,0:T(8,128)(2,1)} copy(bf16[256,3584]{1,0:T(8,128)(2,1)S(1)} %copy-done) | data formatting | bytes 3670016
  42.2 0.0 copy-done.1
  42.2 0.7 %copy.16 = f32[1,4,128,128]{3,2,1,0:T(8,128)} copy(f32[1,4,128,128]{3,2,1,0:T(8,128)S(1)} %copy-done.1) | data formatting | bytes 524288
Async XLA Ops:
  37.9 3.0 %copy-start = (bf16[256,3584]{1,0:T(8,128)(2,1)S(1)}, bf16[256,3584]{1,0:T(8,128)(2,1)}, u32[]{:S(2)}) copy-start(bf16[256,3584]{1,0:T(8,128)(2,1)} %get-tuple-element.7) | copy-start | bytes 5505028
  40.9 1.2 %copy-start.1 = (f32[1,4,128,128]{3,2,1,0:T(8,128)S(1)}, f32[1,4,128,128]{3,2,1,0:T(8,128)}, u32[]{:S(2)}) copy-start(f32[1,4,128,128]{3,2,1,0:T(8,128)} %get-tuple-element.8) | copy-start | bytes 786436

commit v2 on v1

--- a/solution.py
+++ b/solution.py
@@ -9,6 +9,7 @@
 
 CAP = 4
 CORES = 2
+TILES = (1792, 896, 512, 256, 128)
 MESH = pl.DeviceIdType.MESH
 F32 = jnp.float32
 BF16 = jnp.bfloat16
@@ -25,7 +26,7 @@
 def kernel(
     n_t, n_d, rows_ref, cols_ref, owner_ref, gate_hbm, up_hbm, go_hbm, w_hbm, dv_ref,
     gg_hbm, gu_hbm, dg_hbm,
-    gate_v, up_v, slope_v, act_v, go_v, w_v, acc_v, all_hid_v, go_col_v, hid_v, term_v, send_v, recv_v, corr_v, comb_v, own_v,
+    gate_v, up_v, slope_v, act_v, go_v, w_v, acc_v, all_hid_v, go_col_v, hid_v, term_v, send_v, recv_v, mix_v, comb_v, own_v,
     in_sem, w_sem, out_sem, dg_sem, sib_sem, cs_sem, cr_sem, fs_sem, fr_sem, rs_sem, rr_sem,
 ):
     tok, ff = gate_v.shape
@@ -35,7 +36,7 @@
     n_y = n_t // CORES
     chunks = w_sem.shape[0]
     wide = depth // chunks
-    tile = widest(ff, (512, 256, 128))
+    tile = widest(ff, TILES)
     tiles = ff // tile
     me_t = lax.axis_index("tensor")
     me_d = lax.axis_index("dp")
@@ -71,6 +72,7 @@
     pl.semaphore_wait(barrier, 1 + (n_y - 1) + (n_d - 1))
 
     cross, forward = {}, {}
+    early = chunks - 2
     for c in range(chunks):
         span = pl.ds(c * wide, wide)
         for off in range(1, n_y):
@@ -87,7 +89,7 @@
 
     gate_in.wait()
     up_in.wait()
-    strip = 64
+    strip = tok
     strips = tok // strip
 
     def factors(step, carry):
@@ -102,7 +104,7 @@
         all_hid_v[lax.div(step, strips), rows] = (act * up).astype(BF16)
         return carry
 
-    lax.fori_loop(0, strips * (ff // side), factors, 0, unroll=2)
+    lax.fori_loop(0, strips * (ff // side), factors, 0)
 
     row = [lax.rem(rows_ref[k], ff // side) for k in range(blocks)]
     col = [cols_ref[k] for k in range(blocks)]
@@ -130,8 +132,17 @@
     for k in range(blocks):
         hid_v[k] = all_hid_v[row[k]].astype(F32).T.astype(BF16)
 
-    def partial_sum(c, j):
-        span = pl.ds(c * wide, wide)
+    for k in range(blocks):
+        for k2 in range(blocks):
+            spot = (slice(k * side, (k + 1) * side), slice(k2 * side, (k2 + 1) * side))
+            if k2 == k:
+                mix_v[spot] = dv_ref[k2]
+            else:
+                same = (row[k2] == row[k]).astype(jnp.int32).astype(F32)
+                mix_v[spot] = (same * dv_ref[k2].astype(F32)).astype(BF16)
+
+    def partial_sum(c, count, j):
+        span = pl.ds(c * wide, count * wide)
         part = pl.ds(pl.multiple_of(j * tile, tile), tile)
         return lax.dot_general(go_v[:, span], w_v[part, span], NT, preferred_element_type=F32)
 
@@ -140,12 +151,11 @@
             go_col_v[i] = go_v[:, i * side:(i + 1) * side]
 
     def chunk_step(c):
-        by_column(c)
         w_in[c].wait()
 
         def body(j, carry):
             part = pl.ds(pl.multiple_of(j * tile, tile), tile)
-            got = partial_sum(c, j)
+            got = partial_sum(c, 1, j)
             if c == 0:
                 acc_v[:, part] = got
             else:
@@ -170,7 +180,9 @@
         else:
             for off in range(1, n_y):
                 forward[off, c - 1].wait_recv()
-            chunk_step(c - 1)
+            by_column(c - 1)
+            if c - 1 < early:
+                chunk_step(c - 1)
     for off in range(1, n_y):
         forward[off, chunks - 1].wait_recv()
     by_column(chunks - 1)
@@ -190,14 +202,10 @@
             device_id={"dp": peer}, device_id_type=MESH))
         scatter[-1].start()
 
-    for k in range(blocks):
-        corr_v[k] = lax.dot_general(go_col_v[col[k]], dv_ref[k], NT, preferred_element_type=F32)
-    for k in range(blocks):
-        total = corr_v[k]
-        for k2 in range(blocks):
-            if k2 != k:
-                total = total + (row[k2] == row[k]).astype(jnp.int32).astype(F32) * corr_v[k2]
-        comb_v[k] = total
+    picked = jnp.concatenate([go_col_v[col[k]] for k in range(blocks)], axis=1)
+    added = lax.dot_general(picked, mix_v[...], NT, preferred_element_type=F32)
+    for k in range(blocks):
+        comb_v[k] = added[:, k * side:(k + 1) * side]
     comb_v[blocks] = jnp.zeros((tok, side), F32)
 
     def outputs(j):
@@ -205,10 +213,11 @@
         return (pltpu.make_async_copy(gate_v.at[:, part], gg_hbm.at[:, part], out_sem.at[0, j]),
                 pltpu.make_async_copy(up_v.at[:, part], gu_hbm.at[:, part], out_sem.at[1, j]))
 
-    w_in[chunks - 1].wait()
+    for c in range(early, chunks):
+        w_in[c].wait()
 
     def last(j, carry):
-        got = partial_sum(chunks - 1, j)
+        got = partial_sum(early, chunks - early, j)
         for i in range(tile // side):
             part = pl.ds(pl.multiple_of(j * tile + i * side, side), side)
             which = j * (tile // side) + i
@@ -258,7 +267,7 @@
     blocks, side = delta_values.shape[0], delta_values.shape[1]
     chunks = 4
     n_y = n_t // CORES
-    tiles = ff // widest(ff, (512, 256, 128))
+    tiles = ff // widest(ff, TILES)
     smem = pl.BlockSpec(memory_space=pltpu.SMEM)
     anywhere = pl.BlockSpec(memory_space=pl.ANY)
     vmem = pl.BlockSpec(memory_space=pltpu.VMEM)
@@ -286,7 +295,7 @@
             pltpu.VMEM((blocks + 1, side, side), F32),
             pltpu.VMEM((n_d * CAP, side, side), BF16),
             pltpu.VMEM((n_d - 1, CAP, side, side), BF16),
-            pltpu.VMEM((blocks, tok, side), F32),
+            pltpu.VMEM((blocks * side, blocks * side), BF16),
             pltpu.VMEM((blocks + 1, tok, side), F32),
             pltpu.VMEM((1, CAP, side, side), F32),
             dma((3,)),
@@ -302,7 +311,7 @@
             dma((n_d - 1,)),
         ],
         compiler_params=pltpu.CompilerParams(
-            collective_id=0, has_side_effects=True, vmem_limit_bytes=60 * 2**20
+            collective_id=0, has_side_effects=True, vmem_limit_bytes=56 * 2**20
         ),
     )(delta_rows, delta_cols, delta_owner, gate_pre, up_pre, grad_out, down_weight, delta_values)
 

time: 43 us -> 38.5 us (0.90)
  the two profiles are of different devices: /device:TPU:0 before, /device:TPU:11 now
where the time goes in v2:
time: 38.5 us; the launch traced here: 38.3 us
  Pallas kernels  32.8 us (85%)
  local copies, waits for them, and re-layouts  4.92 us (13%)
  between operations  0.65 us (2%)
    pallas_call x1, Pallas kernels, local(): pl.pallas_call(functools.partial(kernel, n_t, n_d), out_shape=(jax.ShapeD...  32.8 us
    unnamed x7, local copies, waits for them, and re-layouts  4.92 us

profile of v2, /device:TPU:11, one launch (start us, length us, event | category | flops | bytes accessed | tf_op | source)
XLA Modules:
  0.0 38.3 jit_solution(9884371570963436243)
XLA Ops:
  0.6 32.8 %shard_map.103 = (bf16[256,3584]{1,0:T(8,128)(2,1)}, bf16[256,3584]{1,0:T(8,128)(2,1)}, f32[1,4,128,128]{3,2,1,0:T(8,128)}) custom-call(s32[8]{0:T(128)} %rows_ref.1, s32[8]{0:T(128)} %cols_ref.1, s32[8]{0:T(128)} %owner_ref.1, bf16[256,3584]{1,0:T(8,128)(2,1)} %gate_hbm.1, bf16[256,3584]{1,0:T(8,128)(2,1)} %up_hbm.1, bf16[64,4096]{1,0:T(8,128)(2,1)} %go_hbm.1, ...), custom_call_target="tpu_custom_call" | custom-call | tf_op jit(solution)/shard_map/pallas_call | solution.py:275
  33.4 0.0 copy-start
  33.4 3.0 %copy.14 = bf16[256,3584]{1,0:T(8,128)(2,1)} copy(bf16[256,3584]{1,0:T(8,128)(2,1)} %get-tuple-element.6) | data formatting | bytes 3670016
  36.4 0.0 copy-done
  36.4 0.0 copy-start.1
  36.4 1.2 %copy.15 = bf16[256,3584]{1,0:T(8,128)(2,1)} copy(bf16[256,3584]{1,0:T(8,128)(2,1)S(1)} %copy-done) | data formatting | bytes 3670016
  37.6 0.0 copy-done.1
  37.6 0.7 %copy.16 = f32[1,4,128,128]{3,2,1,0:T(8,128)} copy(f32[1,4,128,128]{3,2,1,0:T(8,128)S(1)} %copy-done.1) | data formatting | bytes 524288
Async XLA Ops:
  33.4 3.0 %copy-start = (bf16[256,3584]{1,0:T(8,128)(2,1)S(1)}, bf16[256,3584]{1,0:T(8,128)(2,1)}, u32[]{:S(2)}) copy-start(bf16[256,3584]{1,0:T(8,128)(2,1)} %get-tuple-element.7) | copy-start | bytes 5505028
  36.4 1.2 %copy-start.1 = (f32[1,4,128,128]{3,2,1,0:T(8,128)S(1)}, f32[1,4,128,128]{3,2,1,0:T(8,128)}, u32[]{:S(2)}) copy-start(f32[1,4,128,128]{3,2,1,0:T(8,128)} %get-tuple-element.8) | copy-start | bytes 786436

commit v3 on v2

--- a/solution.py
+++ b/solution.py
@@ -60,7 +60,6 @@
     for c in range(chunks):
         span = pl.ds(c * wide, wide)
         w_in.append(pltpu.make_async_copy(w_hbm.at[:, span], w_v.at[:, span], w_sem.at[c]))
-        w_in[-1].start()
 
     barrier = pltpu.get_barrier_semaphore()
     pl.semaphore_signal(barrier, inc=1, device_id={"tensor": sibling}, device_id_type=MESH)
@@ -86,6 +85,8 @@
         send_sem=sib_sem.at[0], recv_sem=sib_sem.at[1],
         device_id={"tensor": sibling}, device_id_type=MESH)
     to_sibling.start()
+    for copy in w_in:
+        copy.start()
 
     gate_in.wait()
     up_in.wait()

time: 38.5 us -> 38.6 us (level)
  no operation moved by 1% of the time
where the time goes in v3:
time: 38.6 us; the launch traced here: 38.4 us
  Pallas kernels  32.8 us (85%)
  local copies, waits for them, and re-layouts  4.92 us (13%)
  between operations  0.65 us (2%)
    pallas_call x1, Pallas kernels, local(): pl.pallas_call(functools.partial(kernel, n_t, n_d), out_shape=(jax.ShapeD...  32.8 us
    unnamed x7, local copies, waits for them, and re-layouts  4.92 us

profile of v3, /device:TPU:11, one launch (start us, length us, event | category | flops | bytes accessed | tf_op | source)
XLA Modules:
  0.0 38.4 jit_solution(7851065488092778293)
XLA Ops:
  0.6 32.8 %shard_map.103 = (bf16[256,3584]{1,0:T(8,128)(2,1)}, bf16[256,3584]{1,0:T(8,128)(2,1)}, f32[1,4,128,128]{3,2,1,0:T(8,128)}) custom-call(s32[8]{0:T(128)} %rows_ref.1, s32[8]{0:T(128)} %cols_ref.1, s32[8]{0:T(128)} %owner_ref.1, bf16[256,3584]{1,0:T(8,128)(2,1)} %gate_hbm.1, bf16[256,3584]{1,0:T(8,128)(2,1)} %up_hbm.1, bf16[64,4096]{1,0:T(8,128)(2,1)} %go_hbm.1, ...), custom_call_target="tpu_custom_call" | custom-call | tf_op jit(solution)/shard_map/pallas_call | solution.py:276
  33.5 0.0 copy-start
  33.5 3.0 %copy.14 = bf16[256,3584]{1,0:T(8,128)(2,1)} copy(bf16[256,3584]{1,0:T(8,128)(2,1)} %get-tuple-element.6) | data formatting | bytes 3670016
  36.5 0.0 copy-done
  36.5 0.0 copy-start.1
  36.5 1.2 %copy.15 = bf16[256,3584]{1,0:T(8,128)(2,1)} copy(bf16[256,3584]{1,0:T(8,128)(2,1)S(1)} %copy-done) | data formatting | bytes 3670016
  37.7 0.0 copy-done.1
  37.7 0.7 %copy.16 = f32[1,4,128,128]{3,2,1,0:T(8,128)} copy(f32[1,4,128,128]{3,2,1,0:T(8,128)S(1)} %copy-done.1) | data formatting | bytes 524288
Async XLA Ops:
  33.5 3.0 %copy-start = (bf16[256,3584]{1,0:T(8,128)(2,1)S(1)}, bf16[256,3584]{1,0:T(8,128)(2,1)}, u32[]{:S(2)}) copy-start(bf16[256,3584]{1,0:T(8,128)(2,1)} %get-tuple-element.7) | copy-start | bytes 5505028
  36.5 1.2 %copy-start.1 = (f32[1,4,128,128]{3,2,1,0:T(8,128)S(1)}, f32[1,4,128,128]{3,2,1,0:T(8,128)}, u32[]{:S(2)}) copy-start(f32[1,4,128,128]{3,2,1,0:T(8,128)} %get-tuple-element.8) | copy-start | bytes 786436
